TPU v7x, 1024 devices: a whole 4x8x16 slice. The times are simulated.
1024 devices in a mesh: dp: 4 (over y_hi), expert: 32 (over z, core), tensor: 8 (over x, y_lo).
Axes of the slice: x: 4, y: 8 (y_hi: 4, y_lo: 2; y = y_hi * 2 + y_lo), z: 16, core: 2. Of those that a mesh axis runs over, the one named last changes fastest.
Arguments:
- out_grad: bfloat16 [16384, 7168], P(('dp', 'expert'), 'tensor'), may hold values from -6 to 6
- expert_ids: int32 [16384, 2], P(('dp', 'expert')), may hold values from 0 to 63, all different within a row; in each aligned block of 128 rows (0 to 127, 128 to 255, ...) at most 6 rows name the same one
- gate_probs: float32 [16384, 2], P(('dp', 'expert')), may hold values from 0.1 to 1
- expert_down: bfloat16 [64, 2432, 7168], P('expert', 'dp', 'tensor'), may hold values from -0.0625 to 0.0625
- saved_gate: bfloat16 [64, 768, 2432], P('expert', 'tensor', 'dp'), may hold values from -6 to 6
- saved_up: bfloat16 [64, 768, 2432], P('expert', 'tensor', 'dp'), may hold values from -6 to 6
Outputs:
- grad_gate: bfloat16 [64, 768, 2432], P('expert', 'tensor', 'dp')
- grad_up: bfloat16 [64, 768, 2432], P('expert', 'tensor', 'dp')
Inputs may be any that keep to these rules, and one draw needn't show every extreme that they name: `expert_ids`: within each group of 128 consecutive tokens (the tokens of one device), no expert is named by more than 6 entries, a bound that some block reaches; a token's two experts differ.
All inputs are finite; a program needn't handle non-finite values.
Results may differ from a plain program's by a relative error of at most 0.019.
Values may be sent and summed in bfloat16 or wider, within the bound.
A program may use at most 32 MiB of HBM per device.

v0:
```python
import jax
import jax.numpy as jnp
from jax import lax
from jax.sharding import PartitionSpec as P


def shards(out_grad, expert_ids, gate_probs, expert_down, saved_gate, saved_up):
    tok_rows, features = out_grad.shape
    local_experts = expert_down.shape[0]
    expert_count = lax.axis_size("expert")
    groups = lax.axis_size("dp") * expert_count
    all_experts = local_experts * expert_count
    share_rows = saved_gate.shape[1]
    capacity = share_rows * lax.axis_size("tensor") // groups
    flat_ids = expert_ids.reshape(-1)
    onehot = (flat_ids[:, None] == jnp.arange(all_experts, dtype=jnp.int32)[None, :]).astype(
        jnp.int32
    )
    slot_rank = jnp.sum((jnp.cumsum(onehot, axis=0) - 1) * onehot, axis=1)
    scaled = (
        gate_probs.reshape(-1, 1) * jnp.repeat(out_grad, 2, axis=0).astype(jnp.float32)
    ).astype(jnp.bfloat16)
    target = flat_ids * capacity + slot_rank
    outbox = jnp.zeros((all_experts * capacity, features), jnp.bfloat16).at[target].set(scaled)
    outbox = outbox.reshape(expert_count, local_experts, capacity, features)
    arrived = lax.all_to_all(outbox, "expert", split_axis=0, concat_axis=0, tiled=True)
    partial_value = jnp.einsum(
        "dsjcf,jhf->jdsch",
        lax.all_gather(arrived[None], "dp", axis=0, tiled=True),
        expert_down,
        preferred_element_type=jnp.float32,
    )
    partial_value = partial_value.reshape(local_experts, -1, partial_value.shape[-1])
    upstream = lax.psum_scatter(
        partial_value.astype(jnp.bfloat16), "tensor", scatter_dimension=1, tiled=True
    ).astype(jnp.float32)
    pre_gate = saved_gate.astype(jnp.float32)
    pre_up = saved_up.astype(jnp.float32)
    sigma = jax.nn.sigmoid(pre_gate)
    grad_up = (upstream * pre_gate * sigma).astype(jnp.bfloat16)
    grad_gate = (upstream * pre_up * sigma * (1.0 + pre_gate * (1.0 - sigma))).astype(jnp.bfloat16)
    return (grad_gate, grad_up)


def solution(mesh):
    in_specs = (
        P(("dp", "expert"), "tensor"),
        P(("dp", "expert"), None),
        P(("dp", "expert"), None),
        P("expert", "dp", "tensor"),
        P("expert", "tensor", "dp"),
        P("expert", "tensor", "dp"),
    )
    out_specs = (P("expert", "tensor", "dp"), P("expert", "tensor", "dp"))
    return jax.shard_map(shards, mesh=mesh, in_specs=in_specs, out_specs=out_specs, check_vma=False)
```

profile of v0, /device:TPU:1, one launch (start us, length us, event | category | flops | bytes accessed | tf_op | source)
XLA Modules:
  0.0 278.2 jit_solution(10321093053255866513)
XLA Ops:
  7.2 0.9 copy.34
  8.2 0.1 eq.29
  8.3 0.1 eq.25
  8.4 0.7 broadcast_multiply_fusion
  9.1 0.6 reduce-window.6
  9.8 0.2 slice_reduce_fusion
  10.0 0.1 copy.33
  10.1 0.1 mul.49
  10.2 2.1 broadcast_in_dim.12
  12.4 1.8 convert_element_type.38
  14.2 0.1 copy.37
  14.3 0.1 mul.51
  14.4 0.1 fusion.21
  14.5 2.6 scatter_custom_fusion
  17.1 1.3 reshape.62
  18.5 0.5 copy.38
  19.0 60.8 %all_to_all.5 = bf16[32,2,6,896]{3,1,2,0:T(2,128)(2,1)} all-to-all(bf16[32,2,6,896]{3,1,2,0:T(2,128)(2,1)S(1)} %copy.38), channel_id=1, replica_groups=mesh['dp'=4,'expert'=32,'tensor'=8] {'expert'}, dimensions={0} | all-to-all | bytes 1376256 | tf_op jit(solution)/shard_map/all_to_all | solution.py:26
  79.9 59.6 %all-gather.3.cloned.1.call-done = bf16[128,2,6,896]{3,1,2,0:T(2,128)(2,1)} async-done(((bf16[32,2,6,896]{3,1,2,0:T(2,128)(2,1)}), bf16[128,2,6,896]{3,1,2,0:T(2,128)(2,1)}) %all-gather.3.cloned.1.call-update) | async-done | bytes 2752528 | tf_op jit(solution)/shard_map/all_gather | solution.py:29
  139.5 4.3 %fusion.3 = bf16[2,4,32,6,608]{4,2,3,1,0:T(8,128)(2,1)S(1)} fusion(bf16[2,608,896]{2,1,0:T(8,128)(2,1)S(1)} %copy-done, bf16[4,32,2,6,896]{4,2,3,1,0:T(2,128)(2,1)} %bitcast.30), kind=kOutput, calls=%fused_computation.4 | convolution fusion | flops 1674461184 | bytes 6799360 | tf_op jit(solution)/shard_map/dsjcf,jhf->jdsch/dot_general | solution.py:27
  143.8 3.3 %copy.41 = bf16[2,4,32,6,608]{4,0,3,2,1:T(2,128)(2,1)} copy(bf16[2,4,32,6,608]{4,2,3,1,0:T(8,128)(2,1)S(1)} %fusion.3) | data formatting | bytes 3735552 | tf_op jit(solution)/shard_map/convert_element_type | solution.py:35
  147.2 1.3 dynamic-slice
  149.2 120.0 %all-reduce.3.cloned.1.call-done = bf16[2,768,608]{2,0,1:T(2,128)(2,1)} async-done(((bf16[2,768,608]{2,0,1:T(2,128)(2,1)}), bf16[2,768,608]{2,0,1:T(2,128)(2,1)}) %all-reduce.3.cloned.1.call-update) | async-done | bytes 1867792
  269.1 1.1 constant_dynamic-slice_fusion
  270.3 1.0 fusion.16
  (16 shorter events, 0.2 us)
Async XLA Ops:
  7.2 132.4 %copy-start = (bf16[2,608,896]{2,1,0:T(8,128)(2,1)S(1)}, bf16[2,608,896]{2,1,0:T(8,128)(2,1)}, u32[]{:S(2)}) copy-start(bf16[2,608,896]{2,1,0:T(8,128)(2,1)} %param.9) | copy-start | bytes 6537220
  7.2 7.0 %copy-start.3 = (f32[128,2]{0,1:T(2,128)S(1)}, f32[128,2]{0,1:T(2,128)}, u32[]{:S(2)}) copy-start(f32[128,2]{0,1:T(2,128)} %param.8) | copy-start | bytes 3076
  7.2 132.3 %all-gather.3.cloned.1.call-start = ((), (), s32[]{:S(2)}) async-start(), calls=%async_computation.1 | async-start | bytes 3440640 | tf_op jit(solution)/shard_map/all_gather | solution.py:29
  79.8 189.3 %all-reduce.3.cloned.1.call-start = ((), (), s32[]{:S(2)}) async-start(), calls=%async_computation.2 | async-start | bytes 3932160
  147.1 123.1 %copy-start.1 = (bf16[2,96,608]{2,1,0:T(8,128)(2,1)S(1)}, bf16[2,96,608]{2,1,0:T(8,128)(2,1)}, u32[]{:S(2)}) copy-start(bf16[2,96,608]{2,1,0:T(8,128)(2,1)} %param.10) | copy-start | bytes 700420
  147.1 123.1 %copy-start.2 = (bf16[2,96,608]{2,1,0:T(8,128)(2,1)S(1)}, bf16[2,96,608]{2,1,0:T(8,128)(2,1)}, u32[]{:S(2)}) copy-start(bf16[2,96,608]{2,1,0:T(8,128)(2,1)} %param.11) | copy-start | bytes 700420
Sparse Core Ops, SparseCore 0:
  79.9 59.5 all-gather.2
  147.3 121.7 all-reduce.2
where the time goes:
time: 279 us; the launch traced here: 278 us
  waiting for transfers between devices  180 us (65%)
  blocking collectives  60.8 us (22%)
  between operations  14.8 us (5%)
  local copies, waits for them, and re-layouts  13.4 us (5%)
  other arithmetic  5.09 us (2%)
  matrix products  4.32 us (2%)
    unnamed x3, waiting for transfers between devices  120 us
    all_to_all x1, blocking collectives, shards(): lax.all_to_all(outbox, 'expert', split_axis=0, concat_axis=0, tiled=True)  60.8 us
    all_gather x1, waiting for transfers between devices, shards(): lax.all_gather(arrived[None], 'dp', axis=0, tiled=True)  59.6 us
  transfers between devices with their start and end apart: 2, of which 2 were waited for; matrix products, arithmetic and copies ran while one was open for 0% of the time, Pallas kernels for 0%

commit v1 on v0

v1 whole, which is shorter than its diff:
```python
import functools

import jax
import jax.numpy as jnp
from jax import lax
from jax.experimental import pallas as pl
from jax.experimental.pallas import tpu as pltpu
from jax.sharding import PartitionSpec as P

MESH = pl.DeviceIdType.MESH
F32 = jnp.float32
BF16 = jnp.bfloat16
AHEAD = 3


def step_residue(s, steps):
    if steps < 4:
        return s
    half = steps // 2
    p = s // 2
    odd = s - 2 * p
    return (1 - odd) * p + odd * ((steps - p) % steps + half * ((half - p) // half))


def row_labels(shape, dim, cap):
    row = lax.broadcasted_iota(jnp.int32, shape, dim)
    core = (row >= 2 * cap).astype(jnp.int32)
    row = row - 2 * cap * core
    expert = (row >= cap).astype(jnp.int32)
    return core, expert, row - cap * expert


def kernel(
    sizes,
    x_ref, meta_ref, w_ref, gate_ref, up_ref,
    out_gate_ref, out_up_ref,
    x_sib, meta_sib, outbox, rows, part, part_in, half_out, half_in, own_sum,
    fac_gate, fac_up, res_gate, res_up,
    sib_send, sib_recv, z_send, z_recv, y_send, y_recv, f_send, f_recv,
    x_send, x_recv, t_send, t_recv,
):
    nz, ny, nx, cap = sizes
    steps = nz // 2
    slab = 4 * cap
    tok, feat = x_ref.shape
    hid = w_ref.shape[1]
    y = lax.axis_index("dp")
    e = lax.axis_index("expert")
    t = lax.axis_index("tensor")
    z, c = e // 2, e % 2
    x, yl = t // 2, t % 2
    right, left = (y + 1) % ny, (y + ny - 1) % ny
    zh, zm = z // steps, z % steps

    def residue(s):
        return (z + step_residue(s, steps)) % steps

    barrier = pltpu.get_barrier_semaphore()

    def greet(device):
        pl.semaphore_signal(barrier, inc=1, device_id=device, device_id_type=MESH)

    greet({"expert": 2 * z + 1 - c})
    greet({"dp": right})
    greet({"dp": left})
    greet({"tensor": 2 * x + 1 - yl})
    for d in range(1, nx):
        greet({"tensor": 2 * ((x + d) % nx) + yl})

    def greet_z(d, carry):
        greet({"expert": 2 * ((z + d) % nz) + c})
        return carry

    lax.fori_loop(1, nz, greet_z, 0)
    pl.semaphore_wait(barrier, 1 + 2 + 1 + (nx - 1) + (nz - 1))

    sib = {"expert": 2 * z + 1 - c}
    copy_meta = pltpu.make_async_remote_copy(
        meta_ref, meta_sib, sib_send.at[0], sib_recv.at[0], device_id=sib, device_id_type=MESH
    )
    copy_x = pltpu.make_async_remote_copy(
        x_ref, x_sib, sib_send.at[1], sib_recv.at[1], device_id=sib, device_id_type=MESH
    )
    copy_meta.start()
    copy_x.start()

    dims = (nz, slab, tok)
    dest = lax.broadcasted_iota(jnp.int32, dims, 0)
    core, expert, rank = row_labels(dims, 1, cap)
    name = (4 * dest + 2 * c + expert).astype(F32)
    earlier = (
        lax.broadcasted_iota(jnp.int32, (tok, tok), 0)
        < lax.broadcasted_iota(jnp.int32, (tok, tok), 1)
    ).astype(F32).astype(BF16)

    def pick(meta, tokens, which):
        mine = core == which
        first = ((name == meta[0:1, :].reshape(1, 1, tok)) & mine).astype(F32)
        second = ((name == meta[1:2, :].reshape(1, 1, tok)) & mine).astype(F32)
        both = first + second
        count = jnp.dot(
            both.reshape(nz * slab, tok).astype(BF16), earlier, preferred_element_type=F32
        ).reshape(dims)
        here = (count == rank.astype(F32)).astype(F32)
        chosen = both * here
        weight = jnp.sum(
            (first * meta[2:3, :].reshape(1, 1, tok) + second * meta[3:4, :].reshape(1, 1, tok))
            * here,
            axis=2, keepdims=True,
        )
        picked = jnp.dot(
            chosen.reshape(nz * slab, tok).astype(BF16), tokens, preferred_element_type=F32
        )
        return picked.reshape(nz, slab, feat), weight

    rows_a, weight_a = pick(meta_ref[...], x_ref[...], c)
    copy_meta.wait_recv()
    copy_x.wait_recv()
    rows_b, weight_b = pick(meta_sib[...], x_sib[...], 1 - c)
    outbox[...] = ((rows_a + rows_b) * (weight_a + weight_b)).astype(BF16)
    rows[y, zm, zh] = outbox[z]

    def z_copy(s, other):
        to = (z - step_residue(s, steps) + nz + other * steps) % nz
        return pltpu.make_async_remote_copy(
            outbox.at[to], rows.at[y, zm, zh], z_send.at[s, other], z_recv.at[s, zh],
            device_id={"expert": 2 * to + c}, device_id_type=MESH,
        )

    def z_wait(s, h):
        pltpu.make_async_remote_copy(
            outbox.at[0], rows.at[y, residue(s), h], z_send.at[s, 0], z_recv.at[s, h],
            device_id=sib, device_id_type=MESH,
        ).wait_recv()

    def z_start(s):
        @pl.when(s > 0)
        def _():
            z_copy(s, 0).start()

        z_copy(s, 1).start()

    def y_copy(s, side):
        to = (right, left)[side]
        return pltpu.make_async_remote_copy(
            rows.at[y, residue(s)], rows.at[y, residue(s)], y_send.at[s, side], y_recv.at[s, side],
            device_id={"dp": to}, device_id_type=MESH,
        )

    def f_copy(s, side):
        source, to = ((left, right), (right, left))[side]
        return pltpu.make_async_remote_copy(
            rows.at[source, residue(s), side], rows.at[source, residue(s), side],
            f_send.at[s, side], f_recv.at[s, side],
            device_id={"dp": to}, device_id_type=MESH,
        )

    def x_copy(s, d):
        to = (x + d) % nx
        return pltpu.make_async_remote_copy(
            part.at[s, to], part_in.at[s, d - 1], x_send.at[s, d - 1], x_recv.at[s, d - 1],
            device_id={"tensor": 2 * to + yl}, device_id_type=MESH,
        )

    def t_copy(s):
        return pltpu.make_async_remote_copy(
            half_out.at[s], half_in.at[s], t_send.at[s], t_recv.at[s],
            device_id={"tensor": 2 * x + 1 - yl}, device_id_type=MESH,
        )

    def spread(s):
        @pl.when(s > 0)
        def _():
            z_wait(s, zh)

        @pl.when(s == 0)
        def _():
            z_wait(s, 1 - zh)

        @pl.when(s > 0)
        def _():
            z_wait(s, 1 - zh)

        y_copy(s, 0).start()
        y_copy(s, 1).start()

    def forward(s):
        y_copy(s, 0).wait_recv()
        f_copy(s, 0).start()
        y_copy(s, 1).wait_recv()
        f_copy(s, 1).start()

    def multiply(s):
        f_copy(s, 0).wait_recv()
        f_copy(s, 1).wait_recv()
        m = residue(s)
        block = jnp.concatenate(
            [rows[i, m].astype(F32).reshape(2 * slab, feat) for i in range(ny)], axis=0
        ).astype(BF16)
        contract = (((1,), (1,)), ((), ()))
        a = lax.dot_general(block, w_ref[0], contract, preferred_element_type=F32)
        b = lax.dot_general(block, w_ref[1], contract, preferred_element_type=F32)
        _, which, _ = row_labels((2 * ny, slab, hid), 1, cap)
        value = jnp.where(
            which == 1, b.reshape(2 * ny, slab, hid), a.reshape(2 * ny, slab, hid)
        )
        part[s] = value.astype(BF16).reshape(ny, 2, slab, hid)
        for d in range(1, nx):
            x_copy(s, d).start()

    def reduce(s):
        for d in range(1, nx):
            x_copy(s, d).wait_recv()

        def total(h):
            value = part[s, x, h].astype(F32)
            for d in range(nx - 1):
                value = value + part_in[s, d, h].astype(F32)
            return value

        half_out[s] = total(1 - yl).astype(BF16)
        t_copy(s).start()
        own_sum[s] = total(yl)

    def finish(s):
        t_copy(s).wait_recv()
        upstream = own_sum[s] + half_in[s].astype(F32)
        res_gate[s] = upstream * fac_gate[s]
        res_up[s] = upstream * fac_up[s]

    for s in range(min(AHEAD, steps)):
        z_start(jnp.int32(s))

    col = lax.broadcasted_iota(jnp.int32, (slab, 2 * steps * 2 * cap), 1)
    core2, expert2, rank2 = row_labels(col.shape, 0, cap)
    base = expert2 * (steps * 2 * cap) + core2 * cap + rank2
    order = jnp.concatenate(
        [(col == base + 2 * cap * residue(s)).astype(F32) for s in range(steps)], axis=0
    ).astype(BF16)

    def to_slabs(ref):
        return jnp.dot(order, ref[...], preferred_element_type=F32).reshape(steps, slab, hid)

    pre_gate = to_slabs(gate_ref)
    pre_up = to_slabs(up_ref)
    sigma = jax.nn.sigmoid(pre_gate)
    fac_up[...] = pre_gate * sigma
    fac_gate[...] = pre_up * sigma * (1.0 + pre_gate * (1.0 - sigma))

    def step(s, carry):
        @pl.when(s + AHEAD < steps)
        def _():
            z_start(s + AHEAD)

        def stage(lag, body):
            @pl.when((s >= lag) & (s < steps + lag))
            def _():
                body(s - lag)

        stage(0, spread)
        stage(1, forward)
        stage(3, multiply)
        stage(4, reduce)
        stage(5, finish)
        return carry

    lax.fori_loop(0, steps + 5, step, 0)

    def from_slabs(ref):
        value = ref[...].reshape(steps * slab, hid).astype(BF16)
        return lax.dot_general(
            order, value, (((0,), (0,)), ((), ())), preferred_element_type=F32
        ).astype(BF16)

    out_gate_ref[...] = from_slabs(res_gate)
    out_up_ref[...] = from_slabs(res_up)

    copy_meta.wait_send()
    copy_x.wait_send()

    def drain(s, carry):
        @pl.when(s > 0)
        def _():
            z_copy(s, 0).wait_send()

        z_copy(s, 1).wait_send()
        for side in range(2):
            y_copy(s, side).wait_send()
            f_copy(s, side).wait_send()
        for d in range(1, nx):
            x_copy(s, d).wait_send()
        t_copy(s).wait_send()
        return carry

    lax.fori_loop(0, steps, drain, 0)


def shards(out_grad, expert_ids, gate_probs, expert_down, saved_gate, saved_up):
    tok, feat = out_grad.shape
    hid = expert_down.shape[1]
    nz = lax.axis_size("expert") // 2
    ny = lax.axis_size("dp")
    nx = lax.axis_size("tensor") // 2
    cap = saved_gate.shape[1] * 2 * nx // (2 * nz * ny)
    steps, slab = nz // 2, 4 * cap
    assert nx == ny and expert_down.shape[0] == 2
    meta = jnp.concatenate(
        [expert_ids.T.astype(F32), gate_probs.T, jnp.zeros((4, tok), F32)], axis=0
    )
    dma = pltpu.SemaphoreType.DMA
    out_rows = 2 * saved_gate.shape[1]
    out = jax.ShapeDtypeStruct((out_rows, hid), BF16)
    vmem = pl.BlockSpec(memory_space=pltpu.VMEM)
    grad_gate, grad_up = pl.pallas_call(
        functools.partial(kernel, (nz, ny, nx, cap)),
        out_shape=(out, out),
        in_specs=[vmem] * 5,
        out_specs=(vmem, vmem),
        scratch_shapes=[
            pltpu.VMEM((tok, feat), BF16),
            pltpu.VMEM((8, tok), F32),
            pltpu.VMEM((nz, slab, feat), BF16),
            pltpu.VMEM((ny, steps, 2, slab, feat), BF16),
            pltpu.VMEM((steps, ny, 2, slab, hid), BF16),
            pltpu.VMEM((steps, nx - 1, 2, slab, hid), BF16),
            pltpu.VMEM((steps, slab, hid), BF16),
            pltpu.VMEM((steps, slab, hid), BF16),
            pltpu.VMEM((steps, slab, hid), F32),
            pltpu.VMEM((steps, slab, hid), F32),
            pltpu.VMEM((steps, slab, hid), F32),
            pltpu.VMEM((steps, slab, hid), F32),
            pltpu.VMEM((steps, slab, hid), F32),
            dma((2,)), dma((2,)),
            dma((steps, 2)), dma((steps, 2)),
            dma((steps, 2)), dma((steps, 2)),
            dma((steps, 2)), dma((steps, 2)),
            dma((steps, nx - 1)), dma((steps, nx - 1)),
            dma((steps,)), dma((steps,)),
        ],
        compiler_params=pltpu.CompilerParams(
            collective_id=0, has_side_effects=True, vmem_limit_bytes=48 * 1024 * 1024
        ),
    )(
        out_grad, meta, expert_down,
        saved_gate.reshape(out_rows, hid), saved_up.reshape(out_rows, hid),
    )
    return grad_gate.reshape(saved_gate.shape), grad_up.reshape(saved_up.shape)


def solution(mesh):
    in_specs = (
        P(("dp", "expert"), "tensor"),
        P(("dp", "expert"), None),
        P(("dp", "expert"), None),
        P("expert", "dp", "tensor"),
        P("expert", "tensor", "dp"),
        P("expert", "tensor", "dp"),
    )
    out_specs = (P("expert", "tensor", "dp"), P("expert", "tensor", "dp"))
    return jax.shard_map(shards, mesh=mesh, in_specs=in_specs, out_specs=out_specs, check_vma=False)
```

time: 279 us -> 107 us (0.38)
  the two profiles are of different devices: /device:TPU:1 before, /device:TPU:64 now
where the time goes in v1:
time: 107 us
  Pallas kernels  99.2 us (93%)
  local copies, waits for them, and re-layouts  5.9 us (6%)
  other arithmetic  1.43 us (1%)
    pallas_call x1, Pallas kernels, shards(): pl.pallas_call(functools.partial(kernel, (nz, ny, nx, cap)), out_shape=(o...  99.2 us
    unnamed x10, local copies, waits for them, and re-layouts  5.83 us

profile of v1, /device:TPU:64, one launch (start us, length us, event | category | flops | bytes accessed | tf_op | source)
XLA Modules:
  0.0 107.1 jit_solution(2411709675047990335)
XLA Ops:
  0.6 0.1 pad.2.clone
  0.7 0.7 convert_bitcast_fusion
  1.4 0.7 maximum_maximum_fusion.meta_ref
  2.1 0.0 copy-start
  2.1 1.6 %copy-done = bf16[2,608,896]{2,1,0:T(8,128)(2,1)S(1)} copy-done((bf16[2,608,896]{2,1,0:T(8,128)(2,1)S(1)}, bf16[2,608,896]{2,1,0:T(8,128)(2,1)}, u32[]{:S(2)}) %copy-start) | copy-done | bytes 2179096
  3.8 0.0 copy-start.1
  3.8 0.9 copy-done.1
  4.7 0.0 copy-start.2
  4.7 0.9 copy-done.2
  5.6 0.0 copy-start.3
  5.7 0.9 copy-done.3
  6.6 99.2 %shard_map.77 = (bf16[192,608]{1,0:T(8,128)(2,1)S(1)}, bf16[192,608]{1,0:T(8,128)(2,1)S(1)}) custom-call(bf16[128,896]{1,0:T(8,128)(2,1)S(1)} %copy-done.3, f32[8,128]{1,0:T(8,128)S(1)} %maximum_maximum_fusion.meta_ref, bf16[2,608,896]{2,1,0:T(8,128)(2,1)S(1)} %copy-done, bf16[192,608]{1,0:T(8,128)(2,1)S(1)} %bitcast.7, bf16[192,608]{1,0:T(8,128)(2,1)S(1)} %bitcast.8), custom_call_target="tpu_custom_call" | custom-call | tf_op jit(solution)/shard_map/pallas_call | solution.py:314
  105.8 0.7 copy.10
  106.4 0.7 copy.11
  (1 shorter events, 0.0 us)
Async XLA Ops:
  2.1 1.6 %copy-start = (bf16[2,608,896]{2,1,0:T(8,128)(2,1)S(1)}, bf16[2,608,896]{2,1,0:T(8,128)(2,1)}, u32[]{:S(2)}) copy-start(bf16[2,608,896]{2,1,0:T(8,128)(2,1)} %w_ref.1) | copy-start | bytes 6537220
  3.8 0.9 copy-start.1
  4.7 0.9 copy-start.2
  5.6 0.9 copy-start.3

commit v2 on v1

v2 whole, which is shorter than its diff:
```python
import functools

import jax
import jax.numpy as jnp
from jax import lax
from jax.experimental import pallas as pl
from jax.experimental.pallas import tpu as pltpu
from jax.sharding import PartitionSpec as P

MESH = pl.DeviceIdType.MESH
F32 = jnp.float32
BF16 = jnp.bfloat16
AHEAD = 3
FORWARD, MULTIPLY, REDUCE, FINISH = 2, 4, 6, 7


def row_labels(shape, dim, cap):
    row = lax.broadcasted_iota(jnp.int32, shape, dim)
    core = (row >= 2 * cap).astype(jnp.int32)
    row = row - 2 * cap * core
    expert = (row >= cap).astype(jnp.int32)
    return core, expert, row - cap * expert


def kernel(
    sizes,
    x_ref, ids_ref, prob_ref, w_ref, gate_ref, up_ref,
    out_gate_ref, out_up_ref,
    x_both, ids_both, prob_both, w, gate, up,
    outbox, rows, part, part_in, half_out, half_in, own_sum,
    fac_gate, fac_up, res_gate, res_up,
    load, sib_send, sib_recv, z_send, z_recv, y_send, y_recv, f_send, f_recv,
    x_send, x_recv, t_send, t_recv,
):
    nz, ny, nx, cap = sizes
    steps = nz // 2
    slab = 4 * cap
    tok, feat = x_ref.shape
    hid = w_ref.shape[1]
    y = lax.axis_index("dp")
    e = lax.axis_index("expert")
    t = lax.axis_index("tensor")
    z, c = e // 2, e % 2
    x, yl = t // 2, t % 2
    right, left = (y + 1) % ny, (y + ny - 1) % ny
    sib = {"expert": 2 * z + 1 - c}
    pair = {"tensor": 2 * x + 1 - yl}

    barrier = pltpu.get_barrier_semaphore()

    def greet(device):
        pl.semaphore_signal(barrier, inc=1, device_id=device, device_id_type=MESH)

    greet(sib)
    greet({"dp": right})
    greet({"dp": left})
    greet(pair)
    for d in range(1, nx):
        greet({"tensor": 2 * ((x + d) % nx) + yl})

    def greet_z(d, carry):
        greet({"expert": 2 * ((z + d) % nz) + c})
        return carry

    lax.fori_loop(1, nz, greet_z, 0)

    loads = [
        pltpu.make_async_copy(source, to, load.at[i])
        for i, (source, to) in enumerate(
            [
                (ids_ref, ids_both.at[0]), (prob_ref, prob_both.at[0]), (x_ref, x_both.at[0]),
                (w_ref, w), (gate_ref, gate), (up_ref, up),
            ]
        )
    ]
    for copy in loads:
        copy.start()

    dims = (nz, slab, tok)
    dest = lax.broadcasted_iota(jnp.int32, dims, 0)
    core, expert, rank = row_labels(dims, 1, cap)
    name = 4 * dest + 2 * c + expert
    earlier = (
        lax.broadcasted_iota(jnp.int32, (tok, tok), 0)
        < lax.broadcasted_iota(jnp.int32, (tok, tok), 1)
    ).astype(F32).astype(BF16)

    def pick(i, which):
        mine = core == which
        first = ((name == ids_both[i, 0:1, :].reshape(1, 1, tok)) & mine).astype(F32)
        second = ((name == ids_both[i, 1:2, :].reshape(1, 1, tok)) & mine).astype(F32)
        both = first + second
        count = jnp.dot(
            both.reshape(nz * slab, tok).astype(BF16), earlier, preferred_element_type=F32
        ).reshape(dims)
        here = (count == rank.astype(F32)).astype(F32)
        weight = (
            first * prob_both[i, 0:1, :].reshape(1, 1, tok)
            + second * prob_both[i, 1:2, :].reshape(1, 1, tok)
        ) * here
        return (both * here).reshape(nz * slab, tok).astype(BF16), weight

    loads[0].wait()
    loads[1].wait()
    chosen_a, weight_a = pick(0, c)

    pl.semaphore_wait(barrier, 1 + 2 + 1 + (nx - 1) + (nz - 1))

    exchange = [
        pltpu.make_async_remote_copy(
            source, to, sib_send.at[i], sib_recv.at[i], device_id=sib, device_id_type=MESH
        )
        for i, (source, to) in enumerate(
            [(ids_ref, ids_both.at[1]), (prob_ref, prob_both.at[1]), (x_ref, x_both.at[1])]
        )
    ]
    for copy in exchange:
        copy.start()
    exchange[0].wait_recv()
    exchange[1].wait_recv()
    chosen_b, weight_b = pick(1, 1 - c)
    weight = jnp.sum(weight_a + weight_b, axis=2, keepdims=True)
    loads[2].wait()
    exchange[2].wait_recv()
    picked = jnp.dot(
        jnp.concatenate([chosen_a, chosen_b], axis=1), x_both[...].reshape(2 * tok, feat),
        preferred_element_type=F32,
    )
    outbox[...] = (picked.reshape(nz, slab, feat) * weight).astype(BF16)

    def z_copy(s, j):
        to = (z + s, z + nz - s - 1)[j] % nz
        return pltpu.make_async_remote_copy(
            outbox.at[to], rows.at[y, s, j], z_send.at[s, j], z_recv.at[s, j],
            device_id={"expert": 2 * to + c}, device_id_type=MESH,
        )

    def z_start(s):
        @pl.when(s > 0)
        def _():
            z_copy(s, 0).start()

        z_copy(s, 1).start()

    def y_copy(s, j, side):
        return pltpu.make_async_remote_copy(
            rows.at[y, s, j], rows.at[y, s, j], y_send.at[s, j, side], y_recv.at[s, j, side],
            device_id={"dp": (right, left)[side]}, device_id_type=MESH,
        )

    def f_copy(s, j):
        source, to = ((left, right), (right, left))[j]
        return pltpu.make_async_remote_copy(
            rows.at[source, s, j], rows.at[source, s, j], f_send.at[s, j], f_recv.at[s, j],
            device_id={"dp": to}, device_id_type=MESH,
        )

    def x_copy(s, d):
        to = (x + d) % nx
        return pltpu.make_async_remote_copy(
            part.at[s, to], part_in.at[s, d - 1], x_send.at[s, d - 1], x_recv.at[s, d - 1],
            device_id={"tensor": 2 * to + yl}, device_id_type=MESH,
        )

    def t_copy(m):
        return pltpu.make_async_remote_copy(
            half_out.at[m], half_in.at[m], t_send.at[m], t_recv.at[m],
            device_id=pair, device_id_type=MESH,
        )

    def place(s, j):
        at = (z + nz - s, z + s + 1)[j] % nz
        return at // steps, at % steps

    def spread(s):
        @pl.when(s > 0)
        def _():
            z_copy(s, 0).wait_recv()

        for j in range(2):
            if j == 1:
                z_copy(s, 1).wait_recv()
            for side in range(2):
                y_copy(s, j, side).start()

    def forward(s):
        for j in range(2):
            y_copy(s, j, j).wait_recv()
            f_copy(s, j).start()

    def multiply(s):
        for j in range(2):
            y_copy(s, j, 1 - j).wait_recv()
        for j in range(2):
            f_copy(s, j).wait_recv()
        block = jnp.concatenate(
            [rows[i, s].astype(F32).reshape(2 * slab, feat) for i in range(ny)], axis=0
        ).astype(BF16)
        contract = (((1,), (1,)), ((), ()))
        a = lax.dot_general(block, w[0], contract, preferred_element_type=F32)
        b = lax.dot_general(block, w[1], contract, preferred_element_type=F32)
        _, which, _ = row_labels((2 * ny, slab, hid), 1, cap)
        value = jnp.where(
            which == 1, b.reshape(2 * ny, slab, hid), a.reshape(2 * ny, slab, hid)
        )
        part[s] = value.astype(BF16).reshape(ny, 2, slab, hid)
        for d in range(1, nx):
            x_copy(s, d).start()

    def reduce(s):
        for d in range(1, nx):
            x_copy(s, d).wait_recv()
        for j in range(2):
            half, m = place(s, j)
            value = part[s, x, j].astype(F32)
            for d in range(nx - 1):
                value = value + part_in[s, d, j].astype(F32)

            @pl.when(half == yl)
            def _():
                own_sum[m] = value

            @pl.when(half != yl)
            def _():
                half_out[m] = value.astype(BF16)
                t_copy(m).start()

    def finish(s):
        for j in range(2):
            half, m = place(s, j)

            @pl.when(half == yl)
            def _():
                t_copy(m).wait_recv()
                upstream = own_sum[m] + half_in[m].astype(F32)
                res_gate[m] = upstream * fac_gate[m]
                res_up[m] = upstream * fac_up[m]

    rows[y, 0, 0] = outbox[z]
    for s in range(min(AHEAD, steps)):
        z_start(jnp.int32(s))

    col = lax.broadcasted_iota(jnp.int32, (slab, 2 * steps * 2 * cap), 1)
    core2, expert2, rank2 = row_labels(col.shape, 0, cap)
    base = expert2 * (steps * 2 * cap) + core2 * cap + rank2
    order = jnp.concatenate(
        [(col == base + 2 * cap * m).astype(F32) for m in range(steps)], axis=0
    ).astype(BF16)

    def factors():
        def to_slabs(ref):
            return jnp.dot(order, ref[...], preferred_element_type=F32).reshape(steps, slab, hid)

        for copy in loads[3:]:
            copy.wait()
        pre_gate = to_slabs(gate)
        pre_up = to_slabs(up)
        sigma = jax.nn.sigmoid(pre_gate)
        fac_up[...] = pre_gate * sigma
        fac_gate[...] = pre_up * sigma * (1.0 + pre_gate * (1.0 - sigma))

    def step(s, carry):
        @pl.when(s + AHEAD < steps)
        def _():
            z_start(s + AHEAD)

        def stage(lag, body):
            @pl.when((s >= lag) & (s < steps + lag))
            def _():
                body(s - lag)

        stage(0, spread)
        stage(FORWARD, forward)

        @pl.when(s == 1)
        def _():
            factors()

        stage(MULTIPLY, multiply)
        stage(REDUCE, reduce)
        stage(FINISH, finish)
        return carry

    lax.fori_loop(0, steps + FINISH, step, 0)

    def from_slabs(ref):
        value = ref[...].reshape(steps * slab, hid).astype(BF16)
        return lax.dot_general(
            order, value, (((0,), (0,)), ((), ())), preferred_element_type=F32
        ).astype(BF16)

    out_gate_ref[...] = from_slabs(res_gate)
    out_up_ref[...] = from_slabs(res_up)

    for copy in exchange:
        copy.wait_send()

    def drain(s, carry):
        @pl.when(s > 0)
        def _():
            z_copy(s, 0).wait_send()

        z_copy(s, 1).wait_send()
        for j in range(2):
            for side in range(2):
                y_copy(s, j, side).wait_send()
            f_copy(s, j).wait_send()
            half, m = place(s, j)

            @pl.when(half != yl)
            def _():
                t_copy(m).wait_send()

        for d in range(1, nx):
            x_copy(s, d).wait_send()
        return carry

    lax.fori_loop(0, steps, drain, 0)


def shards(out_grad, expert_ids, gate_probs, expert_down, saved_gate, saved_up):
    tok, feat = out_grad.shape
    hid = expert_down.shape[1]
    nz = lax.axis_size("expert") // 2
    ny = lax.axis_size("dp")
    nx = lax.axis_size("tensor") // 2
    cap = saved_gate.shape[1] * 2 * nx // (2 * nz * ny)
    steps, slab = nz // 2, 4 * cap
    assert nx == ny and expert_down.shape[0] == 2
    dma = pltpu.SemaphoreType.DMA
    out_rows = 2 * saved_gate.shape[1]
    out = jax.ShapeDtypeStruct((out_rows, hid), BF16)
    vmem = pl.BlockSpec(memory_space=pltpu.VMEM)
    hbm = pl.BlockSpec(memory_space=pl.ANY)
    grad_gate, grad_up = pl.pallas_call(
        functools.partial(kernel, (nz, ny, nx, cap)),
        out_shape=(out, out),
        in_specs=[hbm] * 6,
        out_specs=(vmem, vmem),
        scratch_shapes=[
            pltpu.VMEM((2, tok, feat), BF16),
            pltpu.VMEM((2, 2, tok), jnp.int32),
            pltpu.VMEM((2, 2, tok), F32),
            pltpu.VMEM((2, hid, feat), BF16),
            pltpu.VMEM((out_rows, hid), BF16),
            pltpu.VMEM((out_rows, hid), BF16),
            pltpu.VMEM((nz, slab, feat), BF16),
            pltpu.VMEM((ny, steps, 2, slab, feat), BF16),
            pltpu.VMEM((steps, ny, 2, slab, hid), BF16),
            pltpu.VMEM((steps, nx - 1, 2, slab, hid), BF16),
            pltpu.VMEM((steps, slab, hid), BF16),
            pltpu.VMEM((steps, slab, hid), BF16),
            pltpu.VMEM((steps, slab, hid), F32),
            pltpu.VMEM((steps, slab, hid), F32),
            pltpu.VMEM((steps, slab, hid), F32),
            pltpu.VMEM((steps, slab, hid), F32),
            pltpu.VMEM((steps, slab, hid), F32),
            dma((6,)), dma((3,)), dma((3,)),
            dma((steps, 2)), dma((steps, 2)),
            dma((steps, 2, 2)), dma((steps, 2, 2)),
            dma((steps, 2)), dma((steps, 2)),
            dma((steps, nx - 1)), dma((steps, nx - 1)),
            dma((steps,)), dma((steps,)),
        ],
        compiler_params=pltpu.CompilerParams(
            collective_id=0, has_side_effects=True, vmem_limit_bytes=60 * 1024 * 1024
        ),
    )(
        out_grad, expert_ids.T, gate_probs.T, expert_down,
        saved_gate.reshape(out_rows, hid), saved_up.reshape(out_rows, hid),
    )
    return grad_gate.reshape(saved_gate.shape), grad_up.reshape(saved_up.shape)


def solution(mesh):
    in_specs = (
        P(("dp", "expert"), "tensor"),
        P(("dp", "expert"), None),
        P(("dp", "expert"), None),
        P("expert", "dp", "tensor"),
        P("expert", "tensor", "dp"),
        P("expert", "tensor", "dp"),
    )
    out_specs = (P("expert", "tensor", "dp"), P("expert", "tensor", "dp"))
    return jax.shard_map(shards, mesh=mesh, in_specs=in_specs, out_specs=out_specs, check_vma=False)
```

time: 107 us -> 91.4 us (0.85)
  the two profiles are of different devices: /device:TPU:64 before, /device:TPU:1 now
where the time goes in v2:
time: 91.4 us; the launch traced here: 90.4 us
  Pallas kernels  86.4 us (95%)
  local copies, waits for them, and re-layouts  3.32 us (4%)
    pallas_call x1, Pallas kernels, shards(): pl.pallas_call(functools.partial(kernel, (nz, ny, nx, cap)), out_shape=(o...  86.4 us
    unnamed x2, local copies, waits for them, and re-layouts  3.32 us

profile of v2, /device:TPU:1, one launch (start us, length us, event | category | flops | bytes accessed | tf_op | source)
XLA Modules:
  0.0 90.4 jit_solution(7723643437273674862)
XLA Ops:
  0.6 86.4 %shard_map.77 = (bf16[192,608]{1,0:T(8,128)(2,1)}, bf16[192,608]{1,0:T(8,128)(2,1)}) custom-call(bf16[128,896]{1,0:T(8,128)(2,1)} %x_ref.1, s32[2,128]{1,0:T(2,128)} %bitcast.10, f32[2,128]{1,0:T(2,128)} %bitcast.11, bf16[2,608,896]{2,1,0:T(8,128)(2,1)} %w_ref.1, bf16[192,608]{1,0:T(8,128)(2,1)} %bitcast.6, bf16[192,608]{1,0:T(8,128)(2,1)} %bitcast.7), custom_call_target="tpu_custom_call" | custom-call | tf_op jit(solution)/shard_map/pallas_call | solution.py:335
  87.0 1.7 %copy.10 = bf16[2,96,608]{2,1,0:T(8,128)(2,1)} copy(bf16[2,96,608]{2,1,0:T(8,128)(2,1)} %bitcast.9) | data formatting | bytes 466944
  88.7 1.7 %copy.11 = bf16[2,96,608]{2,1,0:T(8,128)(2,1)} copy(bf16[2,96,608]{2,1,0:T(8,128)(2,1)} %bitcast.8) | data formatting | bytes 466944

commit v3 on v2

--- a/solution.py
+++ b/solution.py
@@ -10,8 +10,8 @@
 MESH = pl.DeviceIdType.MESH
 F32 = jnp.float32
 BF16 = jnp.bfloat16
-AHEAD = 3
-FORWARD, MULTIPLY, REDUCE, FINISH = 2, 4, 6, 7
+AHEAD = 4
+FORWARD, MULTIPLY, REDUCE, FINISH = 2, 4, 7, 9
 
 
 def row_labels(shape, dim, cap):
@@ -30,7 +30,7 @@
     outbox, rows, part, part_in, half_out, half_in, own_sum,
     fac_gate, fac_up, res_gate, res_up,
     load, sib_send, sib_recv, z_send, z_recv, y_send, y_recv, f_send, f_recv,
-    x_send, x_recv, t_send, t_recv,
+    x_send, x_recv, t_send, t_recv, ready,
 ):
     nz, ny, nx, cap = sizes
     steps = nz // 2
@@ -58,11 +58,11 @@
     for d in range(1, nx):
         greet({"tensor": 2 * ((x + d) % nx) + yl})
 
-    def greet_z(d, carry):
-        greet({"expert": 2 * ((z + d) % nz) + c})
+    def greet_above(i, carry):
+        greet({"expert": 2 * i + c})
         return carry
 
-    lax.fori_loop(1, nz, greet_z, 0)
+    lax.fori_loop(z + 1, nz, greet_above, 0)
 
     loads = [
         pltpu.make_async_copy(source, to, load.at[i])
@@ -104,7 +104,7 @@
     loads[1].wait()
     chosen_a, weight_a = pick(0, c)
 
-    pl.semaphore_wait(barrier, 1 + 2 + 1 + (nx - 1) + (nz - 1))
+    pl.semaphore_wait(barrier, 1 + 2 + 1 + (nx - 1) + z)
 
     exchange = [
         pltpu.make_async_remote_copy(
@@ -116,6 +116,14 @@
     ]
     for copy in exchange:
         copy.start()
+
+    def answer_below(i, carry):
+        pl.semaphore_signal(
+            ready.at[z], inc=1, device_id={"expert": 2 * i + c}, device_id_type=MESH
+        )
+        return carry
+
+    lax.fori_loop(0, z, answer_below, 0)
     exchange[0].wait_recv()
     exchange[1].wait_recv()
     chosen_b, weight_b = pick(1, 1 - c)
@@ -128,24 +136,29 @@
     )
     outbox[...] = (picked.reshape(nz, slab, feat) * weight).astype(BF16)
 
+    def z_to(s, j):
+        return (z + s, z + nz - s - 1)[j] % nz
+
     def z_copy(s, j):
-        to = (z + s, z + nz - s - 1)[j] % nz
+        to = z_to(s, j)
         return pltpu.make_async_remote_copy(
             outbox.at[to], rows.at[y, s, j], z_send.at[s, j], z_recv.at[s, j],
             device_id={"expert": 2 * to + c}, device_id_type=MESH,
         )
 
-    def z_start(s):
-        @pl.when(s > 0)
+    def z_start(s, j):
+        to = z_to(s, j)
+
+        @pl.when(to > z)
         def _():
-            z_copy(s, 0).start()
-
-        z_copy(s, 1).start()
+            pl.semaphore_wait(ready.at[to], 1)
+
+        z_copy(s, j).start()
 
     def y_copy(s, j, side):
         return pltpu.make_async_remote_copy(
             rows.at[y, s, j], rows.at[y, s, j], y_send.at[s, j, side], y_recv.at[s, j, side],
-            device_id={"dp": (right, left)[side]}, device_id_type=MESH,
+            device_id={"dp": (y + 1 + side * (ny - 2)) % ny}, device_id_type=MESH,
         )
 
     def f_copy(s, j):
@@ -176,12 +189,12 @@
         @pl.when(s > 0)
         def _():
             z_copy(s, 0).wait_recv()
-
-        for j in range(2):
-            if j == 1:
-                z_copy(s, 1).wait_recv()
-            for side in range(2):
-                y_copy(s, j, side).start()
+            for side in (c, 1 - c):
+                y_copy(s, 0, side).start()
+
+        z_copy(s, 1).wait_recv()
+        for side in (c, 1 - c):
+            y_copy(s, 1, side).start()
 
     def forward(s):
         for j in range(2):
@@ -204,8 +217,8 @@
             which == 1, b.reshape(2 * ny, slab, hid), a.reshape(2 * ny, slab, hid)
         )
         part[s] = value.astype(BF16).reshape(ny, 2, slab, hid)
-        for d in range(1, nx):
-            x_copy(s, d).start()
+        for i in (2, 1, 3):
+            x_copy(s, i + c * (nx - 2 * i)).start()
 
     def reduce(s):
         for d in range(1, nx):
@@ -236,9 +249,32 @@
                 res_gate[m] = upstream * fac_gate[m]
                 res_up[m] = upstream * fac_up[m]
 
+    def drain(s):
+        @pl.when(s > 0)
+        def _():
+            z_copy(s, 0).wait_send()
+
+        z_copy(s, 1).wait_send()
+        for j in range(2):
+            for side in range(2):
+                y_copy(s, j, side).wait_send()
+            f_copy(s, j).wait_send()
+            half, m = place(s, j)
+
+            @pl.when(half != yl)
+            def _():
+                t_copy(m).wait_send()
+
+        for d in range(1, nx):
+            x_copy(s, d).wait_send()
+
     rows[y, 0, 0] = outbox[z]
+    for side in (c, 1 - c):
+        y_copy(0, 0, side).start()
+    for s in range(1, min(AHEAD, steps)):
+        z_start(jnp.int32(s), 0)
     for s in range(min(AHEAD, steps)):
-        z_start(jnp.int32(s))
+        z_start(jnp.int32(s), 1)
 
     col = lax.broadcasted_iota(jnp.int32, (slab, 2 * steps * 2 * cap), 1)
     core2, expert2, rank2 = row_labels(col.shape, 0, cap)
@@ -262,7 +298,8 @@
     def step(s, carry):
         @pl.when(s + AHEAD < steps)
         def _():
-            z_start(s + AHEAD)
+            z_start(s + AHEAD, 0)
+            z_start(s + AHEAD, 1)
 
         def stage(lag, body):
             @pl.when((s >= lag) & (s < steps + lag))
@@ -279,6 +316,7 @@
         stage(MULTIPLY, multiply)
         stage(REDUCE, reduce)
         stage(FINISH, finish)
+        stage(FINISH, drain)
         return carry
 
     lax.fori_loop(0, steps + FINISH, step, 0)
@@ -294,28 +332,6 @@
 
     for copy in exchange:
         copy.wait_send()
-
-    def drain(s, carry):
-        @pl.when(s > 0)
-        def _():
-            z_copy(s, 0).wait_send()
-
-        z_copy(s, 1).wait_send()
-        for j in range(2):
-            for side in range(2):
-                y_copy(s, j, side).wait_send()
-            f_copy(s, j).wait_send()
-            half, m = place(s, j)
-
-            @pl.when(half != yl)
-            def _():
-                t_copy(m).wait_send()
-
-        for d in range(1, nx):
-            x_copy(s, d).wait_send()
-        return carry
-
-    lax.fori_loop(0, steps, drain, 0)
 
 
 def shards(out_grad, expert_ids, gate_probs, expert_down, saved_gate, saved_up):
@@ -360,7 +376,7 @@
             dma((steps, 2, 2)), dma((steps, 2, 2)),
             dma((steps, 2)), dma((steps, 2)),
             dma((steps, nx - 1)), dma((steps, nx - 1)),
-            dma((steps,)), dma((steps,)),
+            dma((steps,)), dma((steps,)), pltpu.SemaphoreType.REGULAR((nz,)),
         ],
         compiler_params=pltpu.CompilerParams(
             collective_id=0, has_side_effects=True, vmem_limit_bytes=60 * 1024 * 1024

time: 91.4 us -> 88.3 us (0.966)
  the two profiles are of different devices: /device:TPU:1 before, /device:TPU:16 now
where the time goes in v3:
time: 88.3 us; the launch traced here: 88 us
  Pallas kernels  84.1 us (95%)
  local copies, waits for them, and re-layouts  3.32 us (4%)
    pallas_call x1, Pallas kernels, shards(): pl.pallas_call(functools.partial(kernel, (nz, ny, nx, cap)), out_shape=(o...  84.1 us
    unnamed x2, local copies, waits for them, and re-layouts  3.32 us

profile of v3, /device:TPU:16, one launch (start us, length us, event | category | flops | bytes accessed | tf_op | source)
XLA Modules:
  0.0 88.0 jit_solution(14335314917188572189)
XLA Ops:
  0.6 84.1 %shard_map.77 = (bf16[192,608]{1,0:T(8,128)(2,1)}, bf16[192,608]{1,0:T(8,128)(2,1)}) custom-call(bf16[128,896]{1,0:T(8,128)(2,1)} %x_ref.1, s32[2,128]{1,0:T(2,128)} %bitcast.10, f32[2,128]{1,0:T(2,128)} %bitcast.11, bf16[2,608,896]{2,1,0:T(8,128)(2,1)} %w_ref.1, bf16[192,608]{1,0:T(8,128)(2,1)} %bitcast.6, bf16[192,608]{1,0:T(8,128)(2,1)} %bitcast.7), custom_call_target="tpu_custom_call" | custom-call | tf_op jit(solution)/shard_map/pallas_call | solution.py:351
  84.7 1.7 %copy.10 = bf16[2,96,608]{2,1,0:T(8,128)(2,1)} copy(bf16[2,96,608]{2,1,0:T(8,128)(2,1)} %bitcast.9) | data formatting | bytes 466944
  86.4 1.7 %copy.11 = bf16[2,96,608]{2,1,0:T(8,128)(2,1)} copy(bf16[2,96,608]{2,1,0:T(8,128)(2,1)} %bitcast.8) | data formatting | bytes 466944

commit v4 on v3

--- a/solution.py
+++ b/solution.py
@@ -306,8 +306,8 @@
             def _():
                 body(s - lag)
 
+        stage(FORWARD, forward)
         stage(0, spread)
-        stage(FORWARD, forward)
 
         @pl.when(s == 1)
         def _():

time: 88.3 us -> 87.6 us (level)
  the two profiles are of different devices: /device:TPU:16 before, /device:TPU:8 now
where the time goes in v4:
time: 87.6 us; the launch traced here: 87.4 us
  Pallas kernels  83.4 us (95%)
  local copies, waits for them, and re-layouts  3.32 us (4%)
    pallas_call x1, Pallas kernels, shards(): pl.pallas_call(functools.partial(kernel, (nz, ny, nx, cap)), out_shape=(o...  83.4 us
    unnamed x2, local copies, waits for them, and re-layouts  3.32 us

profile of v4, /device:TPU:8, one launch (start us, length us, event | category | flops | bytes accessed | tf_op | source)
XLA Modules:
  0.0 87.4 jit_solution(9065044686822830368)
XLA Ops:
  0.6 83.4 %shard_map.77 = (bf16[192,608]{1,0:T(8,128)(2,1)}, bf16[192,608]{1,0:T(8,128)(2,1)}) custom-call(bf16[128,896]{1,0:T(8,128)(2,1)} %x_ref.1, s32[2,128]{1,0:T(2,128)} %bitcast.10, f32[2,128]{1,0:T(2,128)} %bitcast.11, bf16[2,608,896]{2,1,0:T(8,128)(2,1)} %w_ref.1, bf16[192,608]{1,0:T(8,128)(2,1)} %bitcast.6, bf16[192,608]{1,0:T(8,128)(2,1)} %bitcast.7), custom_call_target="tpu_custom_call" | custom-call | tf_op jit(solution)/shard_map/pallas_call | solution.py:351
  84.1 1.7 %copy.10 = bf16[2,96,608]{2,1,0:T(8,128)(2,1)} copy(bf16[2,96,608]{2,1,0:T(8,128)(2,1)} %bitcast.9) | data formatting | bytes 466944
  85.7 1.7 %copy.11 = bf16[2,96,608]{2,1,0:T(8,128)(2,1)} copy(bf16[2,96,608]{2,1,0:T(8,128)(2,1)} %bitcast.8) | data formatting | bytes 466944
